TPU v7x, 512 devices: a whole 4x8x8 slice. The times are simulated.
512 devices in a mesh: row: 16 (over y, core), col: 32 (over z, x).
Axes of the slice: x: 4, y: 8, z: 8, core: 2. Of those that a mesh axis runs over, the one named last changes fastest.
Arguments:
- grad_out: bfloat16 [1024, 8192], P('col', 'row'), may hold values from -4 to 4
- saved_input: bfloat16 [1024, 53248], P('row', 'col'), may hold values from -2 to 2
- codes: bfloat16 [8192, 53248], P('row', 'col'), may hold values from -127 to 127, as said below
- exponents: int32 [8192], P('row'), may hold values from -14 to -11
Outputs:
- input_grad: bfloat16 [1024, 53248], P('row', 'col')
- weight_grad: bfloat16 [8192, 53248], P('row', 'col')
Inputs may be any that keep to these rules, and one draw needn't show every extreme that they name: `codes`: every entry is a whole number.
All inputs are finite; a program needn't handle non-finite values.
Results may differ from a plain program's by a relative error of at most 0.001.
Values may be sent and summed in bfloat16 or wider, within the bound.
A program may use at most 64 MiB of HBM per device.

v0:
```python
import jax
import jax.numpy as jnp
from jax import lax
from jax.sharding import PartitionSpec as P


def local(grad_out, saved_input, codes, exponents):
    scales = jnp.exp2(exponents.astype(jnp.float32)).astype(jnp.bfloat16)
    out_rows = lax.all_gather(grad_out, "col", axis=0, tiled=True)
    weight_side = codes * scales[:, None]
    grad_block = out_rows
    weight_grad = lax.dot_general(
        grad_block,
        lax.all_gather(saved_input, "row", axis=0, tiled=True),
        (((0,), (0,)), ((), ())),
        preferred_element_type=jnp.float32,
    ).astype(jnp.bfloat16)
    grad_block = out_rows
    input_grad = lax.psum_scatter(
        jnp.dot(grad_block, weight_side, preferred_element_type=jnp.float32),
        "row",
        scatter_dimension=0,
        tiled=True,
    ).astype(jnp.bfloat16)
    return (input_grad, weight_grad)


def solution(mesh):
    in_specs = (P("col", "row"), P("row", "col"), P("row", "col"), P("row"))
    out_specs = (P("row", "col"), P("row", "col"))
    return jax.shard_map(local, mesh=mesh, in_specs=in_specs, out_specs=out_specs, check_vma=False)
```

profile of v0, /device:TPU:1, one launch (start us, length us, event | category | flops | bytes accessed | tf_op | source)
XLA Modules:
  0.0 220.6 jit_solution(10742467712566058823)
XLA Ops:
  7.2 0.0 all-gather.3.cloned.1.call-start
  7.2 0.7 all-gather.3.cloned.1.call-update
  7.9 0.0 all-gather.5.cloned.1.call-start
  7.9 0.7 all-gather.5.cloned.1.call-update
  8.6 0.0 reduce-scatter.4.cloned.1.call-start
  8.7 0.7 exponential_convert_fusion
  9.4 85.1 %all-gather.3.cloned.1.call-done = bf16[1024,512]{1,0:T(8,128)(2,1)} async-done(((bf16[32,512]{1,0:T(8,128)(2,1)}), bf16[1024,512]{1,0:T(8,128)(2,1)}) %all-gather.3.cloned.1.call-update) | async-done | bytes 1048592 | tf_op jit(solution)/shard_map/all_gather | solution.py:9
  94.5 6.7 %convolution_bitcast_fusion = f32[1024,1664]{0,1:T(8,128)} fusion(bf16[1024,512]{1,0:T(8,128)(2,1)} %all-gather.3.cloned.1.call-done, bf16[512,1664]{1,0:T(8,128)(2,1)} %param.6, bf16[512]{0:T(512)(128)(2,1)S(1)} %exponential_convert_fusion), kind=kOutput, calls=%fused_computation | convolution fusion | flops 1745682432 | bytes 9569280 | tf_op jit(solution)/shard_map/dot_general | solution.py:20
  101.2 7.6 %copy.8 = f32[1024,1664]{1,0:T(8,128)} copy(f32[1024,1664]{0,1:T(8,128)} %convolution_bitcast_fusion) | data formatting | bytes 13631488
  108.9 0.0 copy-start
  108.9 0.0 reduce-scatter.4.cloned.1.call-update
  108.9 33.5 %all-gather.5.cloned.1.call-done = bf16[1024,1664]{1,0:T(8,128)(2,1)} async-done(((bf16[64,1664]{1,0:T(8,128)(2,1)}), bf16[1024,1664]{1,0:T(8,128)(2,1)}) %all-gather.5.cloned.1.call-update) | async-done | bytes 3407888 | tf_op jit(solution)/shard_map/all_gather | solution.py:14
  142.4 0.0 copy-done
  142.4 5.2 %convolution_convert_fusion = bf16[512,1664]{1,0:T(8,128)(2,1)} fusion(bf16[1024,512]{1,0:T(8,128)(2,1)S(1)} %copy-done, bf16[1024,1664]{1,0:T(8,128)(2,1)} %all-gather.5.cloned.1.call-done), kind=kOutput, calls=%fused_computation.1 | convolution fusion | flops 1745682432 | bytes 6160384 | tf_op jit(solution)/shard_map/dot_general | solution.py:12
  147.7 64.2 %reduce-scatter.4.cloned.1.call-done = f32[64,1664]{1,0:T(8,128)} async-done(((f32[1024,1664]{1,0:T(8,128)}), f32[64,1664]{1,0:T(8,128)}) %reduce-scatter.4.cloned.1.call-update) | async-done | bytes 426000
  211.9 1.3 copy.9
  213.1 0.9 copy.7
Async XLA Ops:
  7.2 87.3 %all-gather.3.cloned.1.call-start = ((), (), s32[]{:S(2)}) async-start(), calls=%async_computation.1 | async-start | bytes 1081344 | tf_op jit(solution)/shard_map/all_gather | solution.py:9
  7.9 134.5 %all-gather.5.cloned.1.call-start = ((), (), s32[]{:S(2)}) async-start(), calls=%async_computation.2 | async-start | bytes 3620864 | tf_op jit(solution)/shard_map/all_gather | solution.py:14
  8.6 203.2 %reduce-scatter.4.cloned.1.call-start = ((), (), s32[]{:S(2)}) async-start(), calls=%async_computation.3 | async-start | bytes 7241728
  108.9 33.5 %copy-start = (bf16[1024,512]{1,0:T(8,128)(2,1)S(1)}, bf16[1024,512]{1,0:T(8,128)(2,1)}, u32[]{:S(2)}) copy-start(bf16[1024,512]{1,0:T(8,128)(2,1)} %all-gather.3.cloned.1.call-done) | copy-start | bytes 3145732
Sparse Core Ops, SparseCore 0:
  11.2 83.2 all-gather.2
  96.6 45.7 all-gather.4
  145.3 66.5 reduce-scatter.3
where the time goes:
time: 222 us; the launch traced here: 221 us
  waiting for transfers between devices  184 us (83%)
  between operations  13.7 us (6%)
  matrix products  12 us (5%)
  local copies, waits for them, and re-layouts  9.79 us (4%)
    all_gather x1, waiting for transfers between devices, local(): out_rows = lax.all_gather(grad_out, 'col', axis=0, tiled=True)  85.1 us
    unnamed x4, waiting for transfers between devices  65.6 us
    all_gather x1, waiting for transfers between devices, local(): lax.all_gather(saved_input, 'row', axis=0, tiled=True)  33.5 us
    unnamed x5, local copies, waits for them, and re-layouts  9.79 us
    dot_general x1, matrix products, local(): jnp.dot(grad_block, weight_side, preferred_element_type=jnp.float32)  6.74 us
    dot_general x1, matrix products, local(): lax.dot_general(grad_block, lax.all_gather(saved_input, 'row', axis=0, ti...  5.25 us
  transfers between devices with their start and end apart: 3, of which 3 were waited for; matrix products, arithmetic and copies ran while one was open for 9% of the time, Pallas kernels for 0%

commit v1 on v0

v1 whole, which is shorter than its diff:
```python
import functools

import jax
import jax.numpy as jnp
from jax import lax
from jax.experimental import pallas as pl
from jax.experimental.pallas import tpu as pltpu
from jax.sharding import PartitionSpec as P

MESH = pl.DeviceIdType.MESH
NY, NZ, NX = 8, 8, 4
CH, FB, TB = 512, 1664, 64
LANES = FB // 128
TOP = 32700.0
COPIES = 80
PARTS = ("go", "si", "mm", "rs")


def encode(value, out):
    top = jnp.max(jnp.max(jnp.abs(value), axis=0), axis=1, keepdims=True)
    code = jnp.ceil(16.0 * jnp.log2(jnp.maximum(top, 1e-30)))
    scale = jnp.exp2(code * (-1.0 / 16)) * TOP
    out[...] = jnp.round(value * scale[None]).astype(jnp.int32).astype(jnp.int16)
    return code


def kernel(g_in, s_in, c_in, e_in, ig_out, wg_out, S, G, W, A, T, GT, Q, WG, IG, TX, RX, lsem, ssem, rsem):
    row, col = lax.axis_index("row"), lax.axis_index("col")
    y, core = lax.div(row, 2), lax.rem(row, 2)
    z, x = lax.div(col, NX), lax.rem(col, NX)
    sent = []

    def device(dy=0, dz=0, dx=0, other=False):
        yy = lax.rem(y + dy + NY, NY)
        cc = 1 - core if other else core
        return (yy * 2 + cc, lax.rem(z + dz + NZ, NZ) * NX + lax.rem(x + dx + NX, NX))

    def send(src, dst, to):
        k = len(sent)
        copy = pltpu.make_async_remote_copy(
            src_ref=src, dst_ref=dst, send_sem=ssem.at[k], recv_sem=rsem.at[k], device_id=to, device_id_type=MESH
        )
        copy.start()
        sent.append(copy)
        return copy

    def local(src, dst, k):
        copy = pltpu.make_async_copy(src, dst, lsem.at[k])
        copy.start()
        return copy

    sibling = device(other=True)
    y_to = {1: device(dy=1), -1: device(dy=-1)}
    z_to = {1: device(dz=1), -1: device(dz=-1)}
    x_to = [device(dx=d) for d in (1, 2, 3)]

    barrier = pltpu.get_barrier_semaphore()
    partners = [sibling, *y_to.values(), *z_to.values(), *x_to]
    for partner in partners:
        pl.semaphore_signal(barrier, inc=1, device_id=partner, device_id_type=MESH)
    pl.semaphore_wait(barrier, len(partners))

    def y_at(d):
        return lax.rem(y + d + 2 * NY, NY)

    def z_at(d):
        return lax.rem(z + d + 2 * NZ, NZ)

    go, si, mm, rs = (p in PARTS for p in ("go", "si", "mm", "rs"))

    mine = pl.ds(pl.multiple_of(lax.rem(x, 2) * 32, 32), 32)
    if go:
        own_g = local(g_in, G.at[z, lax.div(x, 2), mine], 0)
        g_x = [send(g_in, G.at[z, lax.div(x, 2), mine], to) for to in x_to]
    if si:
        s_y = {}
        for h in (0, 1):
            for d in (1, -1):
                s_y[d, h, 0] = send(s_in.at[h], S.at[y * 2 + core, h], y_to[d])
        s_sib = [send(s_in, S.at[y * 2 + core], sibling)]
        own_s = local(s_in, S.at[y * 2 + core], 1)
    if mm:
        codes = send(c_in, W.at[1], sibling)
        own_c = local(c_in, W.at[0], 2)

    def forward_s(step):
        for h in (0, 1):
            for d in (1, -1):
                if (d, h, step) in s_y:
                    s_y[d, h, step].wait_recv()
                    block = S.at[y_at(-d * (step + 1)) * 2 + core, h]
                    if step < 2 or (step == 2 and h == (0 if d == 1 else 1)):
                        s_y[d, h, step + 1] = send(block, block, y_to[d])
                    s_sib.append(send(block, block, sibling))

    g_z = {}

    def forward_g(step):
        for h in (0, 1):
            for d in (1, -1):
                if step == 0:
                    slab = G.at[z, h]
                else:
                    g_z[d, h, step - 1].wait_recv()
                    slab = G.at[z_at(-d * step), h]
                if step < 3 or (step == 3 and h == (0 if d == 1 else 1)):
                    g_z[d, h, step] = send(slab, slab, z_to[d])

    if go:
        own_g.wait()
        for copy in g_x:
            copy.wait_recv()
        forward_g(0)
        if si:
            forward_s(0)
        forward_g(1)
        if si:
            forward_s(1)
        forward_g(2)
        forward_g(3)
        g_z[1, 0, 3].wait_recv()
        g_z[-1, 1, 3].wait_recv()
    elif si:
        forward_s(0)
        forward_s(1)

    if mm:
        scale = jnp.exp2((e_in[...] + 14).astype(jnp.float32)).astype(jnp.bfloat16).reshape(1, 1, CH)
        T[...] = G[:, 1 - core] * scale
        act = send(T, A.at[1], sibling)
        A[0] = G[:, core] * scale
        GT[...] = G[...].reshape(NZ * 128, CH).T
    if si:
        forward_s(2)
    if mm:
        own_c.wait()
        codes.wait_recv()
        act.wait_recv()

        def tile_of_q(at, width):
            cols = pl.ds(at, width)
            tile = jnp.dot(A[0].reshape(NY * TB, CH), W[0, :, cols], preferred_element_type=jnp.float32)
            tile += jnp.dot(A[1].reshape(NY * TB, CH), W[1, :, cols], preferred_element_type=jnp.float32)
            return tile

        @pl.loop(0, LANES // 2)
        def _(j):
            tile = tile_of_q(pl.multiple_of(j * 256, 256), 256)
            for i in (0, 1):
                Q[:, :, j * 2 + i] = tile[:, i * 128 : i * 128 + 128].reshape(NY, 4, 16, 128)

        Q[:, :, LANES - 1] = tile_of_q(128 * (LANES - 1), 128).reshape(NY, 4, 16, 128)

    def tile_of_wg(at, width):
        cols = pl.ds(at, width)
        tile = jnp.dot(GT[...], S[:, :, :, cols].reshape(1024, width), preferred_element_type=jnp.float32)
        WG[:, cols] = tile.astype(jnp.bfloat16)

    def wgrad(part):
        if part == 0:
            own_s.wait()
            for copy in s_sib:
                copy.wait_recv()

        @pl.loop(part * 2, part * 2 + 2)
        def _(j):
            tile_of_wg(pl.multiple_of(j * 256, 256), 256)

        if part == 2:
            tile_of_wg(128 * (LANES - 1), 128)
            return local(WG, wg_out, 3)

    half_lane = lax.broadcasted_iota(jnp.int32, (16, 128), 1) < 64

    def scales(message):
        tile = jnp.exp2(message[2 * LANES].astype(jnp.int32).astype(jnp.float32) * (1.0 / 16)) * (1.0 / TOP)
        turned = pltpu.roll(tile, 64, 1)
        return jnp.where(half_lane, tile, turned), jnp.where(half_lane, turned, tile)

    def decoded(message, group, scale):
        return message[pl.ds(LANES * group, LANES)].astype(jnp.int32).astype(jnp.float32) * scale[None]

    sums = {}

    def reduce_step(step):
        for h in (0, 1):
            for d in (1, -1):
                starts = 0 if h == (0 if d == 1 else 1) else 1
                if step < starts:
                    continue
                to = y_at(d * (4 - step))
                k = 0 if d == 1 else 1
                if step > starts:
                    sums[d, h, step - 1].wait_recv()
                    scale = scales(RX.at[k, h, step - 1])
                codes = []
                for g in (0, 1):
                    value = Q[to, 2 * h + g]
                    if step > starts:
                        value += decoded(RX.at[k, h, step - 1], g, scale[g])
                    codes.append(encode(value, TX.at[k, h, step, pl.ds(LANES * g, LANES)]))
                TX[k, h, step, 2 * LANES] = jnp.where(half_lane, codes[0], codes[1]).astype(jnp.int32).astype(jnp.int16)
                sums[d, h, step] = send(TX.at[k, h, step], RX.at[k, h, step], y_to[d])

    def finish():
        for h in (0, 1):
            for k, d in ((0, 1), (1, -1)):
                sums[d, h, 3].wait_recv()
            scale = [scales(RX.at[k, h, 3]) for k in (0, 1)]
            for g in (0, 1):
                value = Q[y, 2 * h + g]
                for k in (0, 1):
                    value += decoded(RX.at[k, h, 3], g, scale[k][g])
                value = (value * 2.0**-14).astype(jnp.bfloat16)
                for j in range(LANES):
                    IG[pl.ds(32 * h + 16 * g, 16), pl.ds(128 * j, 128)] = value[j]
        return local(IG, ig_out, 4)

    ends = []
    if rs:
        reduce_step(0)
        reduce_step(1)
    if si:
        s_y[1, 0, 3].wait_recv()
        s_y[-1, 1, 3].wait_recv()
        for d, h in ((1, 0), (-1, 1)):
            block = S.at[y_at(4) * 2 + core, h]
            s_sib.append(send(block, block, sibling))
    if mm and si:
        wgrad(0)
    if rs:
        reduce_step(2)
    if mm and si:
        wgrad(1)
    if rs:
        reduce_step(3)
    if mm and si:
        ends.append(wgrad(2))
    if rs:
        ends.append(finish())
    for copy in ends:
        copy.wait()
    for copy in sent:
        copy.wait_send()
    if not mm:
        if si:
            own_s.wait()
            for copy in s_sib:
                copy.wait_recv()
    if mm and not rs:
        pass


def local_part(grad_out, saved_input, codes, exponents):
    any_ = pl.BlockSpec(memory_space=pl.ANY)
    bf16 = jnp.bfloat16
    return pl.pallas_call(
        kernel,
        out_shape=(jax.ShapeDtypeStruct((TB, FB), bf16), jax.ShapeDtypeStruct((CH, FB), bf16)),
        in_specs=[any_, any_, any_, pl.BlockSpec(memory_space=pltpu.VMEM)],
        out_specs=(any_, any_),
        scratch_shapes=[
            pltpu.VMEM((2 * NY, 2, 32, FB), bf16),
            pltpu.VMEM((NZ, 2, TB, CH), bf16),
            pltpu.VMEM((2, CH, FB), bf16),
            pltpu.VMEM((2, NY, TB, CH), bf16),
            pltpu.VMEM((NY, TB, CH), bf16),
            pltpu.VMEM((CH, 2 * NY * TB), bf16),
            pltpu.VMEM((NY, 4, LANES, 16, 128), jnp.float32),
            pltpu.VMEM((CH, FB), bf16),
            pltpu.VMEM((TB, FB), bf16),
            pltpu.VMEM((2, 2, 4, 2 * LANES + 1, 16, 128), jnp.int16),
            pltpu.VMEM((2, 2, 4, 2 * LANES + 1, 16, 128), jnp.int16),
            pltpu.SemaphoreType.DMA((5,)),
            pltpu.SemaphoreType.DMA((COPIES,)),
            pltpu.SemaphoreType.DMA((COPIES,)),
        ],
        compiler_params=pltpu.CompilerParams(collective_id=0, has_side_effects=True, vmem_limit_bytes=48 * 1024 * 1024),
        cost_estimate=pl.CostEstimate(flops=4 * 1024 * CH * FB, bytes_accessed=8_000_000, transcendentals=0),
    )(grad_out, saved_input.reshape(2, 32, FB), codes, exponents)


def solution(mesh):
    in_specs = (P("col", "row"), P("row", "col"), P("row", "col"), P("row"))
    out_specs = (P("row", "col"), P("row", "col"))
    return jax.shard_map(local_part, mesh=mesh, in_specs=in_specs, out_specs=out_specs, check_vma=False)
```

time: 222 us -> 66.8 us (0.30)
  waiting for transfers between devices: 184 us -> 0 us
  Pallas kernels: 0 us -> 60.2 us
  between operations: 13.7 us -> 0.65 us
  matrix products: 12 us -> 0 us
  local copies, waits for them, and re-layouts: 9.79 us -> 5.69 us
    all_gather x2 -> x0, waiting for transfers between devices: 119 us -> none  [the longest x1 85.1 us: local(): out_rows = lax.all_gather(grad_out, 'col', axis=0, tiled=True)]
    unnamed x4 -> x0, waiting for transfers between devices: 65.6 us -> none
    pallas_call x0 -> x1, Pallas kernels: none -> 60.2 us  [local_part(): pl.pallas_call(kernel, out_shape=(jax.ShapeDtypeStruct((TB, FB), bf16), j...]
    dot_general x2 -> x0, matrix products: 12 us -> none  [the longest x1 6.74 us: local(): jnp.dot(grad_block, weight_side, preferred_element_type=jnp.float32)]
    unnamed x5 -> x10, local copies, waits for them, and re-layouts: 9.79 us -> 5.69 us
  transfers between devices with their start and end apart: 3 -> 0, of which waited for: 3 -> 0; matrix products, arithmetic and copies ran while one was open for 9% -> 0% of each run, Pallas kernels for 0% -> 0%
where the time goes in v1:
time: 66.8 us; the launch traced here: 66.5 us
  Pallas kernels  60.2 us (90%)
  local copies, waits for them, and re-layouts  5.69 us (9%)
    pallas_call x1, Pallas kernels, local_part(): pl.pallas_call(kernel, out_shape=(jax.ShapeDtypeStruct((TB, FB), bf16), j...  60.2 us
    unnamed x10, local copies, waits for them, and re-layouts  5.69 us

profile of v1, /device:TPU:1, one launch (start us, length us, event | category | flops | bytes accessed | tf_op | source)
XLA Modules:
  0.0 66.5 jit_solution(13873864376314680141)
XLA Ops:
  0.6 0.0 copy-start
  0.6 1.4 %copy-done = bf16[512,1664]{1,0:T(8,128)(2,1)S(1)} copy-done((bf16[512,1664]{1,0:T(8,128)(2,1)S(1)}, bf16[512,1664]{1,0:T(8,128)(2,1)}, u32[]{:S(2)}) %copy-start) | copy-done | bytes 1703960
  2.1 0.0 copy-start.1
  2.1 0.9 %copy-done.1 = bf16[64,1664]{1,0:T(8,128)(2,1)S(1)} copy-done((bf16[64,1664]{1,0:T(8,128)(2,1)S(1)}, bf16[64,1664]{1,0:T(8,128)(2,1)}, u32[]{:S(2)}) %copy-start.1) | copy-done | bytes 213016
  3.0 0.0 copy-start.2
  3.0 0.8 %copy-done.2 = bf16[32,512]{1,0:T(8,128)(2,1)S(1)} copy-done((bf16[32,512]{1,0:T(8,128)(2,1)S(1)}, bf16[32,512]{1,0:T(8,128)(2,1)}, u32[]{:S(2)}) %copy-start.2) | copy-done | bytes 32792
  3.8 0.0 copy-start.3
  3.8 0.7 %copy-done.3 = s32[512]{0:T(512)S(1)} copy-done((s32[512]{0:T(512)S(1)}, s32[512]{0:T(512)}, u32[]{:S(2)}) %copy-start.3) | copy-done | bytes 2072
  4.5 60.2 %shard_map.59 = (bf16[64,1664]{1,0:T(8,128)(2,1)S(1)}, bf16[512,1664]{1,0:T(8,128)(2,1)S(1)}) custom-call(bf16[32,512]{1,0:T(8,128)(2,1)S(1)} %copy-done.2, bf16[2,32,1664]{2,1,0:T(8,128)(2,1)S(1)} %bitcast.1, bf16[512,1664]{1,0:T(8,128)(2,1)S(1)} %copy-done, s32[512]{0:T(512)S(1)} %copy-done.3), custom_call_target="tpu_custom_call" | custom-call | flops 3489660928 | bytes 8000000 | tf_op jit(solution)/shard_map/pallas_call | solution.py:257
  64.6 0.7 %copy.8 = bf16[64,1664]{1,0:T(8,128)(2,1)} copy(bf16[64,1664]{1,0:T(8,128)(2,1)S(1)} %get-tuple-element.4) | data formatting | bytes 425984
  65.3 1.2 %copy.9 = bf16[512,1664]{1,0:T(8,128)(2,1)} copy(bf16[512,1664]{1,0:T(8,128)(2,1)S(1)} %get-tuple-element.5) | data formatting | bytes 3407872
Async XLA Ops:
  0.6 1.5 %copy-start = (bf16[512,1664]{1,0:T(8,128)(2,1)S(1)}, bf16[512,1664]{1,0:T(8,128)(2,1)}, u32[]{:S(2)}) copy-start(bf16[512,1664]{1,0:T(8,128)(2,1)} %c_in.1) | copy-start | bytes 5111812
  2.1 0.9 %copy-start.1 = (bf16[64,1664]{1,0:T(8,128)(2,1)S(1)}, bf16[64,1664]{1,0:T(8,128)(2,1)}, u32[]{:S(2)}) copy-start(bf16[64,1664]{1,0:T(8,128)(2,1)} %param.5) | copy-start | bytes 638980
  3.0 0.8 %copy-start.2 = (bf16[32,512]{1,0:T(8,128)(2,1)S(1)}, bf16[32,512]{1,0:T(8,128)(2,1)}, u32[]{:S(2)}) copy-start(bf16[32,512]{1,0:T(8,128)(2,1)} %g_in.1) | copy-start | bytes 98308
  3.8 0.7 %copy-start.3 = (s32[512]{0:T(512)S(1)}, s32[512]{0:T(512)}, u32[]{:S(2)}) copy-start(s32[512]{0:T(512)} %e_in.1) | copy-start | bytes 6148

commit v2 on v0

v2 whole, which is shorter than its diff:
```python
import jax
import jax.numpy as jnp
from jax import lax
from jax.experimental import pallas as pl
from jax.experimental.pallas import tpu as pltpu
from jax.sharding import PartitionSpec as P

MESH = pl.DeviceIdType.MESH
NY, NZ, NX = 8, 8, 4
CH, FB, TB = 512, 1664, 64
LANES = FB // 128
TOP = 32700.0
COPIES = 112
ZX = 384
ORDER = (4, 3, -3, 2, -2, 1, -1, 0)
VMEM_LIMIT = 52 * 1000 * 1024


def encode(value, out):
    top = jnp.max(jnp.max(jnp.abs(value), axis=0), axis=1, keepdims=True)
    code = jnp.ceil(16.0 * jnp.log2(jnp.maximum(top, 1e-30)))
    scale = jnp.exp2(code * (-1.0 / 16)) * TOP
    out[pl.ds(0, LANES)] = jnp.round(value * scale[None]).astype(jnp.int32).astype(jnp.int16)
    out[LANES] = jnp.broadcast_to(code, (16, 128)).astype(jnp.int32).astype(jnp.int16)


def decode(message):
    scale = jnp.exp2(message[LANES].astype(jnp.int32).astype(jnp.float32) * (1.0 / 16)) * (1.0 / TOP)
    return message[pl.ds(0, LANES)].astype(jnp.int32).astype(jnp.float32) * scale[None]


def kernel(g_in, s_in, c_in, e_in, ig_out, wg_out, S, G, W, E, A, T, GT, Q, WG, IG, TX, RX, lsem, ssem, rsem):
    row, col = lax.axis_index("row"), lax.axis_index("col")
    y, core = lax.div(row, 2), lax.rem(row, 2)
    z, x = lax.div(col, NX), lax.rem(col, NX)
    sent = []

    def device(dy=0, dz=0, dx=0, other=False):
        yy = lax.rem(y + dy + NY, NY)
        cc = 1 - core if other else core
        return (yy * 2 + cc, lax.rem(z + dz + NZ, NZ) * NX + lax.rem(x + dx + NX, NX))

    def send(src, dst, to):
        k = len(sent)
        copy = pltpu.make_async_remote_copy(
            src_ref=src, dst_ref=dst, send_sem=ssem.at[k], recv_sem=rsem.at[k], device_id=to, device_id_type=MESH
        )
        copy.start()
        sent.append(copy)
        return copy

    def local(src, dst, k):
        copy = pltpu.make_async_copy(src, dst, lsem.at[k])
        copy.start()
        return copy

    sibling = device(other=True)
    y_to = {d: device(dy=d) for d in (1, -1)}
    z_to = {d: device(dz=d) for d in (1, -1, 2, -2, 3, -3, 4)}
    x_to = {d: device(dx=d) for d in (2, 1, -1)}

    own_g = local(g_in, G.at[z, x], 0)
    own_s = local(s_in, S.at[y * 2 + core], 1)
    own_c = local(c_in, W.at[0], 2)
    own_e = local(e_in, E, 3)

    barrier = pltpu.get_barrier_semaphore()
    partners = [sibling, *y_to.values(), *z_to.values(), *x_to.values()]
    for partner in partners:
        pl.semaphore_signal(barrier, inc=1, device_id=partner, device_id_type=MESH)
    pl.semaphore_wait(barrier, len(partners))

    def y_at(d):
        return lax.rem(y + d + 2 * NY, NY)

    def z_at(d):
        return lax.rem(z + d + 2 * NZ, NZ)

    zx, xz = pl.ds(0, ZX), pl.ds(ZX, CH - ZX)
    h_x = {d: send(g_in.at[:, xz], G.at[z, x, :, xz], to) for d, to in x_to.items()}
    g_z = {d: send(g_in.at[:, zx], G.at[z, x, :, zx], to) for d, to in z_to.items()}
    g_x = {(d, 0): send(g_in.at[:, zx], G.at[z, x, :, zx], to) for d, to in x_to.items()}
    s_y = {}
    for h in (0, 1):
        for d in (1, -1):
            s_y[d, h, 0] = send(s_in.at[h], S.at[y * 2 + core, h], y_to[d])
    s_sib = [send(s_in, S.at[y * 2 + core], sibling)]
    codes = send(c_in, W.at[1], sibling)

    def forward_g(d):
        g_z[d].wait_recv()
        chunk = G.at[z_at(-d), x, :, zx]
        for dx, to in x_to.items():
            g_x[dx, d] = send(chunk, chunk, to)

    def forward_s(step, h):
        for d in (1, -1):
            if (d, h, step) in s_y:
                s_y[d, h, step].wait_recv()
                block = S.at[y_at(-d * (step + 1)) * 2 + core, h]
                if step < 2 or (step == 2 and h == (0 if d == 1 else 1)):
                    s_y[d, h, step + 1] = send(block, block, y_to[d])
                s_sib.append(send(block, block, sibling))

    own_g.wait()
    for d in x_to:
        h_x[d].wait_recv()
    h_z = {d: send(G.at[z, :, :, xz], G.at[z, :, :, xz], to) for d, to in z_to.items()}
    for d in (1, -1, 2, -2):
        forward_g(d)
    forward_s(0, 0)
    for d in (3, -3):
        forward_g(d)
    forward_s(0, 1)
    forward_g(4)
    for d in (0, 1, -1, 2, -2, 3, -3):
        for dx in x_to:
            g_x[dx, d].wait_recv()
    forward_s(1, 0)
    forward_s(1, 1)
    for dx in x_to:
        g_x[dx, 4].wait_recv()
    for d in z_to:
        h_z[d].wait_recv()
    own_e.wait()

    scale = jnp.exp2((E[...] + 14).astype(jnp.float32)).astype(jnp.bfloat16).reshape(1, 1, CH)

    def scaled(slots, part, out):
        for k in slots:
            block = G[y_at(ORDER[k]), pl.ds(2 * part, 2)] * scale
            out[k] = block.reshape(TB, CH)

    first, second = range(0, 3), range(3, NY)
    acts = []
    for slots in (first, second):
        at = pl.ds(slots[0], len(slots))
        scaled(slots, 1 - core, T)
        acts.append(send(T.at[at], A.at[1, at], sibling))
    scaled(range(NY), core, A.at[0])
    own_c.wait()
    codes.wait_recv()

    def matmul(slots):
        at, rows = pl.ds(slots[0], len(slots)), len(slots) * TB

        def tile(cols):
            return sum(
                jnp.dot(A[i, at].reshape(rows, CH), W[i, :, cols], preferred_element_type=jnp.float32) for i in (0, 1)
            )

        @pl.loop(0, LANES // 2)
        def _(j):
            value = tile(pl.ds(pl.multiple_of(j * 256, 256), 256))
            for i in (0, 1):
                Q[at, :, j * 2 + i] = value[:, i * 128 : i * 128 + 128].reshape(len(slots), 4, 16, 128)

        Q[at, :, LANES - 1] = tile(pl.ds(128 * (LANES - 1), 128)).reshape(len(slots), 4, 16, 128)

    sums = {}

    def chains(step, longer):
        starts = 0 if longer else 1
        for g in (0, 1):
            for k, d in enumerate((1, -1)):
                h = k if longer else 1 - k
                value = Q[ORDER.index(d * (4 - step) if step else 4), 2 * h + g]
                if step > starts:
                    sums[k, h, g, step - 1].wait_recv()
                    value += decode(RX.at[k, h, g, step - 1])
                out = TX.at[k, h, g, step]
                encode(value, out)
                sums[k, h, g, step] = send(out, RX.at[k, h, g, step], y_to[d])

    def finish():
        for h in (0, 1):
            for g in (0, 1):
                value = Q[NY - 1, 2 * h + g]
                for k in (0, 1):
                    sums[k, h, g, 3].wait_recv()
                    value += decode(RX.at[k, h, g, 3])
                value = (value * 2.0**-14).astype(jnp.bfloat16)
                for j in range(LANES):
                    IG[pl.ds(32 * h + 16 * g, 16), pl.ds(128 * j, 128)] = value[j]
        return local(IG, ig_out, 4)

    def wgrad():
        def tile(cols, width):
            value = jnp.dot(GT[...], S[:, :, :, cols].reshape(1024, width), preferred_element_type=jnp.float32)
            WG[:, cols] = value.astype(jnp.bfloat16)

        @pl.loop(0, LANES // 2)
        def _(j):
            tile(pl.ds(pl.multiple_of(j * 256, 256), 256), 256)

        tile(pl.ds(128 * (LANES - 1), 128), 128)
        return local(WG, wg_out, 5)

    acts[0].wait_recv()
    matmul(first)
    chains(0, True)
    chains(1, False)
    acts[1].wait_recv()
    matmul(second)
    GT[...] = G[...].reshape(1024, CH).T
    chains(1, True)
    forward_s(2, 0)
    chains(2, False)
    forward_s(2, 1)
    chains(2, True)
    forward_s(3, 0)
    forward_s(3, 1)
    chains(3, False)
    chains(3, True)
    own_s.wait()
    for copy in s_sib:
        copy.wait_recv()
    ends = [wgrad(), finish()]
    for copy in ends:
        copy.wait()
    for copy in sent:
        copy.wait_send()


def local_part(grad_out, saved_input, codes, exponents):
    any_, hbm = pl.BlockSpec(memory_space=pl.ANY), pl.BlockSpec(memory_space=pltpu.HBM)
    bf16 = jnp.bfloat16
    message = (2, 2, 2, 4, LANES + 1, 16, 128)
    return pl.pallas_call(
        kernel,
        out_shape=(jax.ShapeDtypeStruct((TB, FB), bf16), jax.ShapeDtypeStruct((CH, FB), bf16)),
        in_specs=[hbm, hbm, hbm, hbm],
        out_specs=(any_, any_),
        scratch_shapes=[
            pltpu.VMEM((2 * NY, 2, 32, FB), bf16),
            pltpu.VMEM((NZ, NX, 32, CH), bf16),
            pltpu.VMEM((2, CH, FB), bf16),
            pltpu.VMEM((CH,), jnp.int32),
            pltpu.VMEM((2, NY, TB, CH), bf16),
            pltpu.VMEM((NY, TB, CH), bf16),
            pltpu.VMEM((CH, 2 * NY * TB), bf16),
            pltpu.VMEM((NY, 4, LANES, 16, 128), jnp.float32),
            pltpu.VMEM((CH, FB), bf16),
            pltpu.VMEM((TB, FB), bf16),
            pltpu.VMEM(message, jnp.int16),
            pltpu.VMEM(message, jnp.int16),
            pltpu.SemaphoreType.DMA((6,)),
            pltpu.SemaphoreType.DMA((COPIES,)),
            pltpu.SemaphoreType.DMA((COPIES,)),
        ],
        compiler_params=pltpu.CompilerParams(collective_id=0, has_side_effects=True, vmem_limit_bytes=VMEM_LIMIT),
        cost_estimate=pl.CostEstimate(flops=4 * 1024 * CH * FB, bytes_accessed=8_000_000, transcendentals=0),
    )(*(pltpu.with_memory_space_constraint(a, pltpu.HBM) for a in (grad_out, saved_input.reshape(2, 32, FB), codes, exponents)))


def solution(mesh):
    in_specs = (P("col", "row"), P("row", "col"), P("row", "col"), P("row"))
    out_specs = (P("row", "col"), P("row", "col"))
    return jax.shard_map(local_part, mesh=mesh, in_specs=in_specs, out_specs=out_specs, check_vma=False)
```

time: 222 us -> 56.5 us (0.25)
  waiting for transfers between devices: 184 us -> 0 us
  Pallas kernels: 0 us -> 53.9 us
  between operations: 13.7 us -> 0.64 us
  matrix products: 12 us -> 0 us
  local copies, waits for them, and re-layouts: 9.79 us -> 1.87 us
    all_gather x2 -> x0, waiting for transfers between devices: 119 us -> none  [the longest x1 85.1 us: local(): out_rows = lax.all_gather(grad_out, 'col', axis=0, tiled=True)]
    unnamed x4 -> x0, waiting for transfers between devices: 65.6 us -> none
    pallas_call x0 -> x1, Pallas kernels: none -> 53.9 us  [local_part(): pl.pallas_call(kernel, out_shape=(jax.ShapeDtypeStruct((TB, FB), bf16), j...]
    dot_general x2 -> x0, matrix products: 12 us -> none  [the longest x1 6.74 us: local(): jnp.dot(grad_block, weight_side, preferred_element_type=jnp.float32)]
    unnamed x5 -> x2, local copies, waits for them, and re-layouts: 9.79 us -> 1.87 us
  transfers between devices with their start and end apart: 3 -> 0, of which waited for: 3 -> 0; matrix products, arithmetic and copies ran while one was open for 9% -> 0% of each run, Pallas kernels for 0% -> 0%
where the time goes in v2:
time: 56.5 us; the launch traced here: 56.4 us
  Pallas kernels  53.9 us (95%)
  local copies, waits for them, and re-layouts  1.87 us (3%)
  between operations  0.64 us (1%)
    pallas_call x1, Pallas kernels, local_part(): pl.pallas_call(kernel, out_shape=(jax.ShapeDtypeStruct((TB, FB), bf16), j...  53.9 us
    unnamed x2, local copies, waits for them, and re-layouts  1.87 us

profile of v2, /device:TPU:1, one launch (start us, length us, event | category | flops | bytes accessed | tf_op | source)
XLA Modules:
  0.0 56.4 jit_solution(4002148341167587529)
XLA Ops:
  0.6 53.9 %shard_map.59 = (bf16[64,1664]{1,0:T(8,128)(2,1)S(1)}, bf16[512,1664]{1,0:T(8,128)(2,1)S(1)}) custom-call(bf16[32,512]{1,0:T(8,128)(2,1)} %g_in.1, bf16[2,32,1664]{2,1,0:T(8,128)(2,1)} %bitcast.1, bf16[512,1664]{1,0:T(8,128)(2,1)} %c_in.1, s32[512]{0:T(512)} %e_in.1), custom_call_target="tpu_custom_call" | custom-call | flops 3489660928 | bytes 8000000 | tf_op jit(solution)/shard_map/pallas_call | solution.py:229
  54.6 0.7 %copy.8 = bf16[64,1664]{1,0:T(8,128)(2,1)} copy(bf16[64,1664]{1,0:T(8,128)(2,1)S(1)} %get-tuple-element.4) | data formatting | bytes 425984
  55.2 1.2 %copy.9 = bf16[512,1664]{1,0:T(8,128)(2,1)} copy(bf16[512,1664]{1,0:T(8,128)(2,1)S(1)} %get-tuple-element.5) | data formatting | bytes 3407872

commit v3 on v2

--- a/solution.py
+++ b/solution.py
@@ -76,13 +76,17 @@
     def z_at(d):
         return lax.rem(z + d + 2 * NZ, NZ)
 
+    def far_half(d, far):
+        return 0 if (d == 1) == far else 1
+
     zx, xz = pl.ds(0, ZX), pl.ds(ZX, CH - ZX)
     h_x = {d: send(g_in.at[:, xz], G.at[z, x, :, xz], to) for d, to in x_to.items()}
     g_z = {d: send(g_in.at[:, zx], G.at[z, x, :, zx], to) for d, to in z_to.items()}
     g_x = {(d, 0): send(g_in.at[:, zx], G.at[z, x, :, zx], to) for d, to in x_to.items()}
     s_y = {}
-    for h in (0, 1):
+    for far in (True, False):
         for d in (1, -1):
+            h = far_half(d, far)
             s_y[d, h, 0] = send(s_in.at[h], S.at[y * 2 + core, h], y_to[d])
     s_sib = [send(s_in, S.at[y * 2 + core], sibling)]
     codes = send(c_in, W.at[1], sibling)
@@ -93,53 +97,55 @@
         for dx, to in x_to.items():
             g_x[dx, d] = send(chunk, chunk, to)
 
-    def forward_s(step, h):
+    def forward_s(step, far):
         for d in (1, -1):
-            if (d, h, step) in s_y:
-                s_y[d, h, step].wait_recv()
-                block = S.at[y_at(-d * (step + 1)) * 2 + core, h]
-                if step < 2 or (step == 2 and h == (0 if d == 1 else 1)):
-                    s_y[d, h, step + 1] = send(block, block, y_to[d])
-                s_sib.append(send(block, block, sibling))
-
+            h = far_half(d, far)
+            s_y[d, h, step].wait_recv()
+            block = S.at[y_at(-d * (step + 1)) * 2 + core, h]
+            if step < (3 if far else 2):
+                s_y[d, h, step + 1] = send(block, block, y_to[d])
+            s_sib.append(send(block, block, sibling))
+
+    own_e.wait()
+    scale = jnp.exp2((E[...] + 14).astype(jnp.float32)).astype(jnp.bfloat16).reshape(1, 1, CH)
     own_g.wait()
     for d in x_to:
         h_x[d].wait_recv()
     h_z = {d: send(G.at[z, :, :, xz], G.at[z, :, :, xz], to) for d, to in z_to.items()}
     for d in (1, -1, 2, -2):
         forward_g(d)
-    forward_s(0, 0)
+    forward_s(0, True)
     for d in (3, -3):
         forward_g(d)
-    forward_s(0, 1)
+    forward_s(0, False)
     forward_g(4)
-    for d in (0, 1, -1, 2, -2, 3, -3):
+
+    def arrived(d):
         for dx in x_to:
             g_x[dx, d].wait_recv()
-    forward_s(1, 0)
-    forward_s(1, 1)
-    for dx in x_to:
-        g_x[dx, 4].wait_recv()
-    for d in z_to:
-        h_z[d].wait_recv()
-    own_e.wait()
-
-    scale = jnp.exp2((E[...] + 14).astype(jnp.float32)).astype(jnp.bfloat16).reshape(1, 1, CH)
-
+        if d:
+            h_z[d].wait_recv()
+
+    for d in (0, 1, -1, 2, -2):
+        arrived(d)
+    forward_s(1, True)
+    for d in (3, -3):
+        arrived(d)
+    forward_s(1, False)
+    arrived(4)
     def scaled(slots, part, out):
         for k in slots:
             block = G[y_at(ORDER[k]), pl.ds(2 * part, 2)] * scale
             out[k] = block.reshape(TB, CH)
 
     first, second = range(0, 3), range(3, NY)
-    acts = []
-    for slots in (first, second):
+    acts = {}
+
+    def exchange(slots):
         at = pl.ds(slots[0], len(slots))
         scaled(slots, 1 - core, T)
-        acts.append(send(T.at[at], A.at[1, at], sibling))
-    scaled(range(NY), core, A.at[0])
-    own_c.wait()
-    codes.wait_recv()
+        acts[slots] = send(T.at[at], A.at[1, at], sibling)
+        scaled(slots, core, A.at[0])
 
     def matmul(slots):
         at, rows = pl.ds(slots[0], len(slots)), len(slots) * TB
@@ -196,22 +202,25 @@
         tile(pl.ds(128 * (LANES - 1), 128), 128)
         return local(WG, wg_out, 5)
 
-    acts[0].wait_recv()
+    exchange(first)
+    own_c.wait()
+    codes.wait_recv()
+    acts[first].wait_recv()
     matmul(first)
     chains(0, True)
     chains(1, False)
-    acts[1].wait_recv()
+    exchange(second)
+    forward_s(2, True)
+    acts[second].wait_recv()
     matmul(second)
+    chains(1, True)
     GT[...] = G[...].reshape(1024, CH).T
-    chains(1, True)
-    forward_s(2, 0)
     chains(2, False)
-    forward_s(2, 1)
+    forward_s(2, False)
     chains(2, True)
-    forward_s(3, 0)
-    forward_s(3, 1)
     chains(3, False)
     chains(3, True)
+    forward_s(3, True)
     own_s.wait()
     for copy in s_sib:
         copy.wait_recv()
@@ -222,13 +231,22 @@
         copy.wait_send()
 
 
+def store(ig_in, wg_in, ig_out, wg_out, sem):
+    copies = [pltpu.make_async_copy(wg_in, wg_out, sem.at[0]), pltpu.make_async_copy(ig_in, ig_out, sem.at[1])]
+    for copy in copies:
+        copy.start()
+    for copy in copies:
+        copy.wait()
+
+
 def local_part(grad_out, saved_input, codes, exponents):
     any_, hbm = pl.BlockSpec(memory_space=pl.ANY), pl.BlockSpec(memory_space=pltpu.HBM)
     bf16 = jnp.bfloat16
     message = (2, 2, 2, 4, LANES + 1, 16, 128)
-    return pl.pallas_call(
+    shapes = (jax.ShapeDtypeStruct((TB, FB), bf16), jax.ShapeDtypeStruct((CH, FB), bf16))
+    grads = pl.pallas_call(
         kernel,
-        out_shape=(jax.ShapeDtypeStruct((TB, FB), bf16), jax.ShapeDtypeStruct((CH, FB), bf16)),
+        out_shape=shapes,
         in_specs=[hbm, hbm, hbm, hbm],
         out_specs=(any_, any_),
         scratch_shapes=[
@@ -251,6 +269,14 @@
         compiler_params=pltpu.CompilerParams(collective_id=0, has_side_effects=True, vmem_limit_bytes=VMEM_LIMIT),
         cost_estimate=pl.CostEstimate(flops=4 * 1024 * CH * FB, bytes_accessed=8_000_000, transcendentals=0),
     )(*(pltpu.with_memory_space_constraint(a, pltpu.HBM) for a in (grad_out, saved_input.reshape(2, 32, FB), codes, exponents)))
+    return pl.pallas_call(
+        store,
+        out_shape=shapes,
+        in_specs=[any_, any_],
+        out_specs=(any_, any_),
+        scratch_shapes=[pltpu.SemaphoreType.DMA((2,))],
+        compiler_params=pltpu.CompilerParams(vmem_limit_bytes=1024 * 1024),
+    )(*grads)
 
 
 def solution(mesh):

time: 56.5 us -> 55.9 us (0.989)
  local copies, waits for them, and re-layouts: 1.87 us -> 0 us
  Pallas kernels: 53.9 us -> 55.1 us
    unnamed x2 -> x0, local copies, waits for them, and re-layouts: 1.87 us -> none
    pallas_call x1 -> x2, Pallas kernels: 53.9 us -> 55.1 us  [the longest x1 53.9 us: local_part(): pl.pallas_call(kernel, out_shape=shapes, in_specs=[hbm, hbm, hbm, hbm], o...]
where the time goes in v3:
time: 55.9 us; the launch traced here: 55.8 us
  Pallas kernels  55.1 us (99%)
  between operations  0.64 us (1%)
    pallas_call x1, Pallas kernels, local_part(): pl.pallas_call(kernel, out_shape=shapes, in_specs=[hbm, hbm, hbm, hbm], o...  53.9 us
    pallas_call x1, Pallas kernels, local_part(): pl.pallas_call(store, out_shape=shapes, in_specs=[any_, any_], out_specs=...  1.26 us

profile of v3, /device:TPU:1, one launch (start us, length us, event | category | flops | bytes accessed | tf_op | source)
XLA Modules:
  0.0 55.8 jit_solution(4038534881248693208)
XLA Ops:
  0.6 53.9 %shard_map.59 = (bf16[64,1664]{1,0:T(8,128)(2,1)S(1)}, bf16[512,1664]{1,0:T(8,128)(2,1)S(1)}) custom-call(bf16[32,512]{1,0:T(8,128)(2,1)} %g_in.1, bf16[2,32,1664]{2,1,0:T(8,128)(2,1)} %bitcast.1, bf16[512,1664]{1,0:T(8,128)(2,1)} %c_in.1, s32[512]{0:T(512)} %e_in.1), custom_call_target="tpu_custom_call" | custom-call | flops 3489660928 | bytes 8000000 | tf_op jit(solution)/shard_map/pallas_call | solution.py:247
  54.5 1.3 %shard_map.60 = (bf16[64,1664]{1,0:T(8,128)(2,1)}, bf16[512,1664]{1,0:T(8,128)(2,1)}) custom-call(bf16[64,1664]{1,0:T(8,128)(2,1)S(1)} %get-tuple-element.4.ig_in, bf16[512,1664]{1,0:T(8,128)(2,1)S(1)} %get-tuple-element.5.wg_in), custom_call_target="tpu_custom_call" | custom-call | tf_op jit(solution)/shard_map/pallas_call | solution.py:272

commit v4 on v3

--- a/solution.py
+++ b/solution.py
@@ -29,7 +29,7 @@
     return message[pl.ds(0, LANES)].astype(jnp.int32).astype(jnp.float32) * scale[None]
 
 
-def kernel(g_in, s_in, c_in, e_in, ig_out, wg_out, S, G, W, E, A, T, GT, Q, WG, IG, TX, RX, lsem, ssem, rsem):
+def kernel(g_in, s_in, c_in, e_in, ig_out, wg_out, S, G, W, E, A, T, GT, Q, WG, TX, RX, lsem, ssem, rsem):
     row, col = lax.axis_index("row"), lax.axis_index("col")
     y, core = lax.div(row, 2), lax.rem(row, 2)
     z, x = lax.div(col, NX), lax.rem(col, NX)
@@ -109,10 +109,12 @@
     own_e.wait()
     scale = jnp.exp2((E[...] + 14).astype(jnp.float32)).astype(jnp.bfloat16).reshape(1, 1, CH)
     own_g.wait()
+    for d in (1, -1):
+        forward_g(d)
     for d in x_to:
         h_x[d].wait_recv()
     h_z = {d: send(G.at[z, :, :, xz], G.at[z, :, :, xz], to) for d, to in z_to.items()}
-    for d in (1, -1, 2, -2):
+    for d in (2, -2):
         forward_g(d)
     forward_s(0, True)
     for d in (3, -3):
@@ -138,7 +140,7 @@
             block = G[y_at(ORDER[k]), pl.ds(2 * part, 2)] * scale
             out[k] = block.reshape(TB, CH)
 
-    first, second = range(0, 3), range(3, NY)
+    first, second, rest = range(0, 1), range(1, 3), range(3, NY)
     acts = {}
 
     def exchange(slots):
@@ -187,8 +189,7 @@
                     value += decode(RX.at[k, h, g, 3])
                 value = (value * 2.0**-14).astype(jnp.bfloat16)
                 for j in range(LANES):
-                    IG[pl.ds(32 * h + 16 * g, 16), pl.ds(128 * j, 128)] = value[j]
-        return local(IG, ig_out, 4)
+                    ig_out[pl.ds(32 * h + 16 * g, 16), pl.ds(128 * j, 128)] = value[j]
 
     def wgrad():
         def tile(cols, width):
@@ -200,21 +201,24 @@
             tile(pl.ds(pl.multiple_of(j * 256, 256), 256), 256)
 
         tile(pl.ds(128 * (LANES - 1), 128), 128)
-        return local(WG, wg_out, 5)
+        return local(WG, wg_out, 4)
 
     exchange(first)
+    exchange(second)
     own_c.wait()
     codes.wait_recv()
     acts[first].wait_recv()
     matmul(first)
     chains(0, True)
-    chains(1, False)
-    exchange(second)
-    forward_s(2, True)
     acts[second].wait_recv()
     matmul(second)
+    chains(1, False)
+    exchange(rest)
+    forward_s(2, True)
+    acts[rest].wait_recv()
+    matmul(rest)
+    GT[...] = G[...].reshape(1024, CH).T
     chains(1, True)
-    GT[...] = G[...].reshape(1024, CH).T
     chains(2, False)
     forward_s(2, False)
     chains(2, True)
@@ -224,7 +228,8 @@
     own_s.wait()
     for copy in s_sib:
         copy.wait_recv()
-    ends = [wgrad(), finish()]
+    ends = [wgrad()]
+    finish()
     for copy in ends:
         copy.wait()
     for copy in sent:
@@ -248,7 +253,7 @@
         kernel,
         out_shape=shapes,
         in_specs=[hbm, hbm, hbm, hbm],
-        out_specs=(any_, any_),
+        out_specs=(pl.BlockSpec(memory_space=pltpu.VMEM), any_),
         scratch_shapes=[
             pltpu.VMEM((2 * NY, 2, 32, FB), bf16),
             pltpu.VMEM((NZ, NX, 32, CH), bf16),
@@ -259,10 +264,9 @@
             pltpu.VMEM((CH, 2 * NY * TB), bf16),
             pltpu.VMEM((NY, 4, LANES, 16, 128), jnp.float32),
             pltpu.VMEM((CH, FB), bf16),
-            pltpu.VMEM((TB, FB), bf16),
             pltpu.VMEM(message, jnp.int16),
             pltpu.VMEM(message, jnp.int16),
-            pltpu.SemaphoreType.DMA((6,)),
+            pltpu.SemaphoreType.DMA((5,)),
             pltpu.SemaphoreType.DMA((COPIES,)),
             pltpu.SemaphoreType.DMA((COPIES,)),
         ],

time: 55.9 us -> 55.4 us (level)
  no operation moved by 1% of the time
where the time goes in v4:
time: 55.4 us; the launch traced here: 55.3 us
  Pallas kernels  54.7 us (99%)
  between operations  0.64 us (1%)
    pallas_call x1, Pallas kernels, local_part(): pl.pallas_call(kernel, out_shape=shapes, in_specs=[hbm, hbm, hbm, hbm], o...  53.4 us
    pallas_call x1, Pallas kernels, local_part(): pl.pallas_call(store, out_shape=shapes, in_specs=[any_, any_], out_specs=...  1.26 us

profile of v4, /device:TPU:1, one launch (start us, length us, event | category | flops | bytes accessed | tf_op | source)
XLA Modules:
  0.0 55.3 jit_solution(10430927843849933616)
XLA Ops:
  0.6 53.4 %shard_map.59 = (bf16[64,1664]{1,0:T(8,128)(2,1)S(1)}, bf16[512,1664]{1,0:T(8,128)(2,1)S(1)}) custom-call(bf16[32,512]{1,0:T(8,128)(2,1)} %g_in.1, bf16[2,32,1664]{2,1,0:T(8,128)(2,1)} %bitcast.1, bf16[512,1664]{1,0:T(8,128)(2,1)} %c_in.1, s32[512]{0:T(512)} %e_in.1), custom_call_target="tpu_custom_call" | custom-call | flops 3489660928 | bytes 8000000 | tf_op jit(solution)/shard_map/pallas_call | solution.py:252
  54.1 1.3 %shard_map.60 = (bf16[64,1664]{1,0:T(8,128)(2,1)}, bf16[512,1664]{1,0:T(8,128)(2,1)}) custom-call(bf16[64,1664]{1,0:T(8,128)(2,1)S(1)} %get-tuple-element.4.ig_in, bf16[512,1664]{1,0:T(8,128)(2,1)S(1)} %get-tuple-element.5.wg_in), custom_call_target="tpu_custom_call" | custom-call | tf_op jit(solution)/shard_map/pallas_call | solution.py:276

commit v5 on v4

--- a/solution.py
+++ b/solution.py
@@ -114,9 +114,9 @@
     for d in x_to:
         h_x[d].wait_recv()
     h_z = {d: send(G.at[z, :, :, xz], G.at[z, :, :, xz], to) for d, to in z_to.items()}
+    forward_s(0, True)
     for d in (2, -2):
         forward_g(d)
-    forward_s(0, True)
     for d in (3, -3):
         forward_g(d)
     forward_s(0, False)

time: 55.4 us -> 55.4 us (level)
  no operation moved by 1% of the time
where the time goes in v5:
time: 55.4 us; the launch traced here: 55.3 us
  Pallas kernels  54.7 us (99%)
  between operations  0.64 us (1%)
    pallas_call x1, Pallas kernels, local_part(): pl.pallas_call(kernel, out_shape=shapes, in_specs=[hbm, hbm, hbm, hbm], o...  53.4 us
    pallas_call x1, Pallas kernels, local_part(): pl.pallas_call(store, out_shape=shapes, in_specs=[any_, any_], out_specs=...  1.26 us

profile of v5, /device:TPU:1, one launch (start us, length us, event | category | flops | bytes accessed | tf_op | source)
XLA Modules:
  0.0 55.3 jit_solution(13086960733906682392)
XLA Ops:
  0.6 53.4 %shard_map.59 = (bf16[64,1664]{1,0:T(8,128)(2,1)S(1)}, bf16[512,1664]{1,0:T(8,128)(2,1)S(1)}) custom-call(bf16[32,512]{1,0:T(8,128)(2,1)} %g_in.1, bf16[2,32,1664]{2,1,0:T(8,128)(2,1)} %bitcast.1, bf16[512,1664]{1,0:T(8,128)(2,1)} %c_in.1, s32[512]{0:T(512)} %e_in.1), custom_call_target="tpu_custom_call" | custom-call | flops 3489660928 | bytes 8000000 | tf_op jit(solution)/shard_map/pallas_call | solution.py:252
  54.1 1.3 %shard_map.60 = (bf16[64,1664]{1,0:T(8,128)(2,1)}, bf16[512,1664]{1,0:T(8,128)(2,1)}) custom-call(bf16[64,1664]{1,0:T(8,128)(2,1)S(1)} %get-tuple-element.4.ig_in, bf16[512,1664]{1,0:T(8,128)(2,1)S(1)} %get-tuple-element.5.wg_in), custom_call_target="tpu_custom_call" | custom-call | tf_op jit(solution)/shard_map/pallas_call | solution.py:276
